TPU v7x, 32 devices: a whole 2x2x4 slice. The times are simulated.
32 devices in a mesh: word: 4 (over x, core), ctx: 8 (over z, y).
Axes of the slice: x: 2, y: 2, z: 4, core: 2. Of those that a mesh axis runs over, the one named last changes fastest.
Arguments:
- counts: int32 [6144, 12288], P('word', 'ctx'), may hold values from 0 to 1800, as said below
- word_vecs: float32 [6144, 300], P(('word', 'ctx')), may hold values from -0.35 to 0.35
- word_bias: float32 [6144], P(('word', 'ctx')), may hold values from 0.5 to 3
- word_accum: float32 [6144, 300], P(('word', 'ctx')), may hold values from 3.2552084e-06 to 0.00016276042
- word_bias_accum: float32 [6144], P(('word', 'ctx')), may hold values from 1 to 30
- ctx_vecs: float32 [12288, 300], P(('ctx', 'word')), may hold values from -0.35 to 0.35
- ctx_bias: float32 [12288], P(('ctx', 'word')), may hold values from 0.5 to 3
- ctx_accum: float32 [12288, 300], P(('ctx', 'word')), may hold values from 6.510417e-06 to 0.00032552084
- ctx_bias_accum: float32 [12288], P(('ctx', 'word')), may hold values from 1 to 30
Outputs:
- new_word_vecs: float32 [6144, 300], P(('word', 'ctx'))
- new_word_bias: float32 [6144], P(('word', 'ctx'))
- new_word_accum: float32 [6144, 300], P(('word', 'ctx'))
- new_word_bias_accum: float32 [6144], P(('word', 'ctx'))
- new_ctx_vecs: float32 [12288, 300], P(('ctx', 'word'))
- new_ctx_bias: float32 [12288], P(('ctx', 'word'))
- new_ctx_accum: float32 [12288, 300], P(('ctx', 'word'))
- new_ctx_bias_accum: float32 [12288], P(('ctx', 'word'))
Inputs may be any that keep to these rules, and one draw needn't show every extreme that they name: counts are non-negative integers, and a count is zero exactly where the word and the context never co-occur.
All inputs are finite; a program needn't handle non-finite values.
Results may differ from a plain program's by a relative error of at most 0.0045.
Values may be sent and summed in bfloat16 or wider, within the bound.
A program may use at most 64 MiB of HBM per device.

v0:
```python
import jax
import jax.numpy as jnp
from jax import lax
from jax.sharding import PartitionSpec as P

count_cap = 100.0
power_law = 0.75
step_rate = 0.2


def weighted_residual(tile_counts, word_rows, ctx_rows, word_bias_rows, ctx_bias_rows):
    values = tile_counts.astype(jnp.float32)
    log_count = jnp.log(jnp.maximum(values, 1.0))
    weight = jnp.where(tile_counts > 0, jnp.minimum((values / count_cap) ** power_law, 1.0), 0.0)
    inner = lax.dot_general(
        word_rows, ctx_rows, (((1,), (1,)), ((), ())), preferred_element_type=jnp.float32
    )
    return weight * (inner + word_bias_rows[:, None] + ctx_bias_rows[None, :] - log_count)


def adagrad(param, accum, grad):
    new_accum = accum + grad * grad
    return (param - step_rate * grad / jnp.sqrt(new_accum), new_accum)


def per_device(
    counts,
    word_vecs,
    word_bias,
    word_accum,
    word_bias_accum,
    ctx_vecs,
    ctx_bias,
    ctx_accum,
    ctx_bias_accum,
):
    word_rows, word_bias_rows = (
        lax.all_gather(word_vecs.astype(jnp.bfloat16), "ctx", axis=0, tiled=True),
        lax.all_gather(word_bias.astype(jnp.bfloat16), "ctx", axis=0, tiled=True),
    )
    ctx_rows, ctx_bias_rows = (
        lax.all_gather(ctx_vecs.astype(jnp.bfloat16), "word", axis=0, tiled=True),
        lax.all_gather(ctx_bias.astype(jnp.bfloat16), "word", axis=0, tiled=True),
    )
    scaled = weighted_residual(
        counts,
        word_rows,
        ctx_rows,
        word_bias_rows.astype(jnp.float32),
        ctx_bias_rows.astype(jnp.float32),
    )
    scaled_low = scaled.astype(jnp.bfloat16)
    word_term = jnp.dot(scaled_low, ctx_rows, preferred_element_type=jnp.float32)
    word_bias_term = jnp.sum(scaled, axis=1)
    ctx_term = lax.dot_general(
        scaled_low, word_rows, (((0,), (0,)), ((), ())), preferred_element_type=jnp.float32
    )
    ctx_bias_term = jnp.sum(scaled, axis=0)
    word_sum, word_bias_sum = (
        lax.psum_scatter(word_term, "ctx", scatter_dimension=0, tiled=True),
        lax.psum_scatter(word_bias_term, "ctx", scatter_dimension=0, tiled=True),
    )
    ctx_sum, ctx_bias_sum = (
        lax.psum_scatter(ctx_term, "word", scatter_dimension=0, tiled=True),
        lax.psum_scatter(ctx_bias_term, "word", scatter_dimension=0, tiled=True),
    )
    all_contexts = counts.shape[1] * lax.axis_size("ctx")
    all_words = counts.shape[0] * lax.axis_size("word")
    word_scale = 2.0 / all_contexts
    ctx_scale = 2.0 / all_words
    new_word_vecs, new_word_accum = adagrad(word_vecs, word_accum, word_scale * word_sum)
    new_word_bias, new_word_bias_accum = adagrad(
        word_bias, word_bias_accum, word_scale * word_bias_sum
    )
    new_ctx_vecs, new_ctx_accum = adagrad(ctx_vecs, ctx_accum, ctx_scale * ctx_sum)
    new_ctx_bias, new_ctx_bias_accum = adagrad(ctx_bias, ctx_bias_accum, ctx_scale * ctx_bias_sum)
    return (
        new_word_vecs,
        new_word_bias,
        new_word_accum,
        new_word_bias_accum,
        new_ctx_vecs,
        new_ctx_bias,
        new_ctx_accum,
        new_ctx_bias_accum,
    )


def solution(mesh):
    return jax.shard_map(
        per_device,
        mesh=mesh,
        in_specs=(
            P("word", "ctx"),
            P(("word", "ctx"), None),
            P(("word", "ctx")),
            P(("word", "ctx"), None),
            P(("word", "ctx")),
            P(("ctx", "word"), None),
            P(("ctx", "word")),
            P(("ctx", "word"), None),
            P(("ctx", "word")),
        ),
        out_specs=(
            P(("word", "ctx"), None),
            P(("word", "ctx")),
            P(("word", "ctx"), None),
            P(("word", "ctx")),
            P(("ctx", "word"), None),
            P(("ctx", "word")),
            P(("ctx", "word"), None),
            P(("ctx", "word")),
        ),
        check_vma=False,
    )
```

profile of v0, /device:TPU:0, one launch (start us, length us, event | category | flops | bytes accessed | tf_op | source)
XLA Modules:
  0.0 213.6 jit_solution(514880483064799508)
XLA Ops:
  7.2 0.0 reduce-scatter.5.cloned.1.call-start
  7.2 0.7 convert_element_type.27
  7.9 1.3 fusion.5
  9.9 0.2 dynamic-update-slice
  10.1 23.1 %all-reduce = bf16[1536]{0:T(1024)(128)(2,1)S(1)} all-reduce(bf16[1536]{0:T(1024)(128)(2,1)S(1)} %dynamic-update-slice), channel_id=1, replica_groups=mesh['word'=4,'ctx'=8] {'ctx'}, use_global_device_ids=true, to_apply=%add | all-reduce | flops 1536 | bytes 6144
  33.3 1.0 convert_element_type.25
  34.2 33.8 %all_gather.12 = bf16[1536,300]{1,0:T(8,128)(2,1)S(1)} all-gather(bf16[192,300]{1,0:T(8,128)(2,1)S(1)} %convert_element_type.25), channel_id=1, replica_groups=mesh['word'=4,'ctx'=8] {'ctx'}, dimensions={0}, use_global_device_ids=true | all-gather | bytes 1036800 | tf_op jit(solution)/shard_map/all_gather | solution.py:38
  68.0 1.0 convert_element_type.26
  69.1 9.4 %all_gather.13 = bf16[1536,300]{0,1:T(8,128)(2,1)S(1)} all-gather(bf16[384,300]{0,1:T(8,128)(2,1)S(1)} %convert_element_type.26), channel_id=1, replica_groups=mesh['word'=4,'ctx'=8] {'word'}, dimensions={0}, use_global_device_ids=true | all-gather | bytes 1152000 | tf_op jit(solution)/shard_map/all_gather | solution.py:42
  78.5 0.7 convert_element_type.29
  79.2 5.1 %all-gather = bf16[4,1,384]{2,1,0:T(2,128)(2,1)S(1)} all-gather(bf16[1,1,384]{2,1,0:T(2,128)(2,1)S(1)} %reshape.21), channel_id=1, replica_groups=mesh['word'=4,'ctx'=8] {'word'}, dimensions={0}, use_global_device_ids=true | all-gather | bytes 3840 | tf_op jit(solution)/shard_map/all_gather | solution.py:43
  84.3 15.0 %fusion.4 = (f32[1536]{0:T(1024)S(1)}, f32[1536]{0:T(1024)S(1)}, bf16[1536,1536]{1,0:T(8,128)(2,1)S(1)}) fusion(f32[1536]{0:T(1024)S(1)} %reshape.23, f32[1536]{0:T(1024)S(1)} %convert_element_type.28, bf16[1536,300]{1,0:T(8,128)(2,1)S(1)} %all_gather.12, bf16[1536,300]{0,1:T(8,128)(2,1)S(1)} %all_gather.13, s32[1536,1536]{1,0:T(8,128)} %param.9), kind=kOutput, calls=%fused_computation.15 | convolution fusion | flops 1446245376 | bytes 16023552 | tf_op jit(solution)/shard_map/dot_general | solution.py:15
  99.4 0.0 copy-start.9
  99.4 2.1 copy-done.9
  101.5 3.0 %fusion = f32[1536,300]{0,1:T(8,128)} fusion(bf16[1536,300]{1,0:T(8,128)(2,1)S(1)} %all_gather.12, bf16[1536,1536]{1,0:T(8,128)(2,1)S(1)} %get-tuple-element.20), kind=kOutput, calls=%fused_computation.2 | convolution fusion | flops 1415577600 | bytes 7483392 | tf_op jit(solution)/shard_map/dot_general | solution.py:55
  104.5 0.0 copy-start.5
  104.5 0.0 copy-start
  104.5 0.0 copy-start.2
  104.5 0.0 copy-start.1
  104.5 0.0 copy-start.3
  104.5 0.0 reduce-scatter.5.cloned.1.call-update
  104.6 0.0 reduce-scatter.3.cloned.1.call-start
  104.6 6.5 %fusion.2 = f32[1536,300]{1,0:T(8,128)} fusion(bf16[1536,300]{0,1:T(8,128)(2,1)S(1)} %all_gather.13, bf16[1536,1536]{1,0:T(8,128)(2,1)} %copy-done.9), kind=kOutput, calls=%fused_computation.4 | convolution fusion | flops 1415577600 | bytes 7483392 | tf_op jit(solution)/shard_map/dot_general | solution.py:53
  111.2 0.0 reduce-scatter.3.cloned.1.call-update
  111.2 0.6 dynamic-slice.3
  113.1 18.9 %all-reduce.1 = f32[1536]{0:T(1024)S(1)} all-reduce(f32[1536]{0:T(1024)S(1)} %get-tuple-element.9), channel_id=3, replica_groups=mesh['word'=4,'ctx'=8] {'ctx'}, use_global_device_ids=true, to_apply=%region_2.3.clone | all-reduce | flops 1536 | bytes 12288
  132.0 6.1 %all-reduce.2 = f32[1536]{0:T(1024)S(1)} all-reduce(f32[1536]{0:T(1024)S(1)} %get-tuple-element.8), channel_id=5, replica_groups=mesh['word'=4,'ctx'=8] {'word'}, use_global_device_ids=true, to_apply=%region_5.6.clone | all-reduce | flops 1536 | bytes 12288
  138.1 0.7 multiply_subtract_fusion.3
  138.7 0.7 multiply_subtract_fusion.2
  139.4 2.1 multiply_subtract_fusion
  141.5 63.4 %reduce-scatter.3.cloned.1.call-done = f32[192,300]{1,0:T(8,128)} async-done(((f32[1536,300]{1,0:T(8,128)}), f32[192,300]{1,0:T(8,128)}) %reduce-scatter.3.cloned.1.call-update) | async-done | bytes 230416 | tf_op jit(solution)/shard_map/reduce_scatter | solution.py:60
  204.9 1.8 multiply_subtract_fusion.1
  (19 shorter events, 0.1 us)
Async XLA Ops:
  7.2 132.2 %reduce-scatter.5.cloned.1.call-start = ((), (), s32[]{:S(2)}) async-start(), calls=%async_computation.3 | async-start | bytes 2334720 | tf_op jit(solution)/shard_map/reduce_scatter | solution.py:64
  99.4 2.1 copy-start.9
  104.5 6.7 %copy-start.8 = (u32[32]{0:T(128)S(1)}, u32[32]{0:T(128)}, u32[]{:S(2)}) copy-start(u32[32]{0:T(128)} %constant.39) | copy-start | bytes 388
  104.5 33.6 %copy-start.6 = (f32[192]{0:T(256)S(1)}, f32[192]{0:T(256)}, u32[]{:S(2)}) copy-start(f32[192]{0:T(256)} %param.11) | copy-start | bytes 2308
  104.5 33.6 %copy-start.7 = (f32[192]{0:T(256)S(1)}, f32[192]{0:T(256)}, u32[]{:S(2)}) copy-start(f32[192]{0:T(256)} %param.13) | copy-start | bytes 2308
  104.5 34.3 %copy-start.4 = (f32[384]{0:T(512)S(1)}, f32[384]{0:T(512)}, u32[]{:S(2)}) copy-start(f32[384]{0:T(512)} %param.15) | copy-start | bytes 4612
  104.5 34.3 %copy-start.5 = (f32[384]{0:T(512)S(1)}, f32[384]{0:T(512)}, u32[]{:S(2)}) copy-start(f32[384]{0:T(512)} %param.17) | copy-start | bytes 4612
  104.5 34.9 %copy-start = (f32[384,300]{0,1:T(8,128)S(1)}, f32[384,300]{0,1:T(8,128)}, u32[]{:S(2)}) copy-start(f32[384,300]{0,1:T(8,128)} %param.14) | copy-start | bytes 1382404
  104.5 34.9 %copy-start.2 = (f32[384,300]{0,1:T(8,128)S(1)}, f32[384,300]{0,1:T(8,128)}, u32[]{:S(2)}) copy-start(f32[384,300]{0,1:T(8,128)} %param.16) | copy-start | bytes 1382404
  104.5 100.4 %copy-start.1 = (f32[192,300]{1,0:T(8,128)S(1)}, f32[192,300]{1,0:T(8,128)}, u32[]{:S(2)}) copy-start(f32[192,300]{1,0:T(8,128)} %param.10) | copy-start | bytes 691204
  104.5 100.4 %copy-start.3 = (f32[192,300]{1,0:T(8,128)S(1)}, f32[192,300]{1,0:T(8,128)}, u32[]{:S(2)}) copy-start(f32[192,300]{1,0:T(8,128)} %param.12) | copy-start | bytes 691204
  104.6 100.4 %reduce-scatter.3.cloned.1.call-start = ((), (), s32[]{:S(2)}) async-start(), calls=%async_computation.2 | async-start | bytes 2654208 | tf_op jit(solution)/shard_map/reduce_scatter | solution.py:60
Sparse Core Ops, SparseCore 0:
  104.7 27.3 reduce-scatter.4
  135.9 68.9 reduce-scatter.2
where the time goes:
time: 214 us
  blocking collectives  96.4 us (45%)
  waiting for transfers between devices  63.5 us (30%)
  matrix products  24.5 us (11%)
  between operations  16.1 us (8%)
  other arithmetic  8.66 us (4%)
  local copies, waits for them, and re-layouts  4.34 us (2%)
    reduce_scatter x1, waiting for transfers between devices, per_device(): lax.psum_scatter(word_term, 'ctx', scatter_dimension=0, tiled=True)  63.4 us
    unnamed x3, blocking collectives  48.1 us
    all_gather x1, blocking collectives, per_device(): lax.all_gather(word_vecs.astype(jnp.bfloat16), 'ctx', axis=0, tiled=True)  33.8 us
    dot_general x1, matrix products, weighted_residual(): lax.dot_general(word_rows, ctx_rows, (((1,), (1,)), ((), ())), preferred_...  15 us
    all_gather x1, blocking collectives, per_device(): lax.all_gather(ctx_vecs.astype(jnp.bfloat16), 'word', axis=0, tiled=True)  9.4 us
    dot_general x1, matrix products, per_device(): jnp.dot(scaled_low, ctx_rows, preferred_element_type=jnp.float32)  6.55 us
    sub x4, other arithmetic, adagrad(): return (param - step_rate * grad / jnp.sqrt(new_accum), new_accum)  5.23 us
    all_gather x1, blocking collectives, per_device(): lax.all_gather(ctx_bias.astype(jnp.bfloat16), 'word', axis=0, tiled=True)  5.14 us
  transfers between devices with their start and end apart: 2, of which 1 were waited for; matrix products, arithmetic and copies ran while one was open for 5% of the time, Pallas kernels for 0%

commit v1 on v0

--- a/solution.py
+++ b/solution.py
@@ -1,6 +1,11 @@
+import functools
+import math
+
 import jax
 import jax.numpy as jnp
 from jax import lax
+from jax.experimental import pallas as pl
+from jax.experimental.pallas import tpu as pltpu
 from jax.sharding import PartitionSpec as P
 
 count_cap = 100.0
@@ -23,7 +28,7 @@
     return (param - step_rate * grad / jnp.sqrt(new_accum), new_accum)
 
 
-def per_device(
+def per_device_plain(
     counts,
     word_vecs,
     word_bias,
@@ -86,9 +91,438 @@
     )
 
 
+MESH = pl.DeviceIdType.MESH
+
+
+def remote(src, dst, send_sem, recv_sem, device):
+    return pltpu.make_async_remote_copy(
+        src_ref=src,
+        dst_ref=dst,
+        send_sem=send_sem,
+        recv_sem=recv_sem,
+        device_id=device,
+        device_id_type=MESH,
+    )
+
+
+def near_first(n):
+    return sorted(range(n), key=lambda d: (min(d, n - d), d))
+
+
+def tile_kernel(
+    n_word,
+    n_ctx,
+    counts_hbm,
+    word_own,
+    ctx_own,
+    word_out,
+    ctx_out,
+    counts,
+    weight,
+    log_count,
+    scaled_low,
+    word_all,
+    word_all_t,
+    ctx_all,
+    own_part,
+    y_out,
+    y_in,
+    z_out,
+    z_in,
+    ctx_part,
+    core_out,
+    core_in,
+    x_out,
+    x_in,
+    count_sem,
+    wz_s,
+    wz_r,
+    wy_s,
+    wy_r,
+    cx_s,
+    cx_r,
+    cc_s,
+    cc_r,
+    ry_s,
+    ry_r,
+    rz_s,
+    rz_r,
+    rc_s,
+    rc_r,
+    rx_s,
+    rx_r,
+):
+    rows, lanes = word_own.shape
+    depth, cols = ctx_own.shape
+    nz, nx = n_ctx // 2, n_word // 2
+    w, c = lax.axis_index("word"), lax.axis_index("ctx")
+    x, core = w // 2, w % 2
+    z, y = c // 2, c % 2
+
+    def ctx_peer(zi, yi):
+        return (w, zi * 2 + yi)
+
+    def word_peer(xi, ci):
+        return (xi * 2 + ci, c)
+
+    def zf(d):
+        return (z + d) % nz
+
+    def zb(d):
+        return (z + nz - d) % nz
+
+    def xf(d):
+        return (x + d) % nx
+
+    def xb(d):
+        return (x + nx - d) % nx
+
+    def word_rows(block):
+        return pl.ds(pl.multiple_of(block * rows, rows), rows)
+
+    def ctx_cols(block):
+        return pl.ds(pl.multiple_of(block * cols, cols), cols)
+
+    z_order = near_first(nz)
+    steps = []
+    for i, d in enumerate(z_order):
+        pair = [(d, True), (d, False)]
+        steps += pair if i < 2 else pair[::-1]
+
+    def block_of(step):
+        d, mine = step
+        return zb(d) * 2 + (y if mine else 1 - y)
+
+    count_copies = []
+    for i, step in enumerate(steps):
+        at = word_rows(block_of(step))
+        copy = pltpu.make_async_copy(counts_hbm.at[at, :], counts.at[at, :], count_sem.at[i])
+        copy.start()
+        count_copies.append(copy)
+
+    barrier = pltpu.get_barrier_semaphore()
+    peers = [ctx_peer(zf(d), y) for d in range(1, nz)] + [ctx_peer(z, 1 - y)]
+    peers += [word_peer(xf(d), core) for d in range(1, nx)] + [word_peer(x, 1 - core)]
+    for peer in peers:
+        pl.semaphore_signal(barrier, inc=1, device_id=peer, device_id_type=MESH)
+    pl.semaphore_wait(barrier, len(peers))
+
+    sends = []
+    wz, wy, cx, cc = {}, {}, {}, {}
+
+    def wy_copy(d, src):
+        at = word_rows(zb(d) * 2 + y)
+        wy[d] = remote(src, word_all.at[at, :], wy_s.at[d], wy_r.at[d], ctx_peer(z, 1 - y))
+        wy[d].start()
+        sends.append(wy[d])
+
+    def cc_copy(d, src):
+        at = ctx_cols(xb(d) * 2 + core)
+        cc[d] = remote(
+            src, ctx_all.at[:depth, at], cc_s.at[d], cc_r.at[d], word_peer(x, 1 - core)
+        )
+        cc[d].start()
+        sends.append(cc[d])
+
+    for d in range(1, nx):
+        cx[d] = remote(
+            ctx_own,
+            ctx_all.at[:depth, ctx_cols(w)],
+            cx_s.at[d - 1],
+            cx_r.at[d - 1],
+            word_peer(xf(d), core),
+        )
+        cx[d].start()
+        sends.append(cx[d])
+    cc_copy(0, ctx_own)
+    wy_copy(0, word_own)
+    for d in z_order[1:]:
+        wz[d] = remote(
+            word_own,
+            word_all.at[word_rows(c), :],
+            wz_s.at[d - 1],
+            wz_r.at[d - 1],
+            ctx_peer(zf(d), y),
+        )
+        wz[d].start()
+        sends.append(wz[d])
+    word_all[word_rows(c), :] = word_own[...]
+    ctx_all[:depth, ctx_cols(w)] = ctx_own[...]
+    ctx_all[depth:, :] = jnp.zeros((lanes - depth, ctx_all.shape[1]), ctx_all.dtype)
+
+    forwards = [("c", d) for d in range(1, nx)] + [("w", d) for d in z_order[1:]]
+
+    def forward():
+        if not forwards:
+            return
+        kind, d = forwards.pop(0)
+        if kind == "c":
+            cx[d].wait_recv()
+            cc_copy(d, ctx_all.at[:depth, ctx_cols(xb(d) * 2 + core)])
+        else:
+            wz[d].wait_recv()
+            wy_copy(d, word_all.at[word_rows(zb(d) * 2 + y), :])
+
+    group = 16
+    log2_cap = math.log2(count_cap)
+    for i, step in enumerate(steps):
+        count_copies[i].wait()
+        base = block_of(step) * rows
+
+        @pl.loop(0, rows // group)
+        def _(r):
+            at = pl.ds(pl.multiple_of(base + r * group, group), group)
+            tile = counts[at, :]
+            log2 = jnp.log2(jnp.maximum(tile.astype(jnp.float32), 1.0))
+            power = jnp.minimum(jnp.exp2(power_law * (log2 - log2_cap)), 1.0)
+            weight[at, :] = jnp.where(tile > 0, power, 0.0)
+            log_count[at, :] = log2 * math.log(2.0)
+
+        if i >= 2:
+            forward()
+    while forwards:
+        forward()
+    for d in range(nx):
+        cc[d].wait_recv()
+
+    ry, rz, rc, rx = {}, {}, {}, {}
+    wait_combine = []
+
+    def combine(d):
+        ry[d].wait_recv()
+        total = own_part[d] + y_in[d].astype(jnp.float32)
+        if d == 0:
+            own_part[d] = total
+        else:
+            z_out[d - 1] = total.astype(jnp.bfloat16)
+            rz[d] = remote(
+                z_out.at[d - 1],
+                z_in.at[d - 1],
+                rz_s.at[d - 1],
+                rz_r.at[d - 1],
+                ctx_peer(zb(d), y),
+            )
+            rz[d].start()
+            sends.append(rz[d])
+
+    done = set()
+    for step in steps:
+        d, mine = step
+        at = word_rows(block_of(step))
+        if not mine:
+            wy[d].wait_recv()
+        block = word_all[at, :]
+        for j in range(n_word):
+            part = pl.ds(j * cols, cols)
+            inner = jnp.dot(block, ctx_all[:, part], preferred_element_type=jnp.float32)
+            scaled = weight[at, part] * (inner - log_count[at, part])
+            scaled_low[at, part] = scaled.astype(jnp.bfloat16)
+        term = lax.dot_general(
+            scaled_low[at, :],
+            ctx_all[...],
+            (((1,), (1,)), ((), ())),
+            preferred_element_type=jnp.float32,
+        )
+        if mine:
+            own_part[d] = term
+        else:
+            y_out[d] = term.astype(jnp.bfloat16)
+            ry[d] = remote(
+                y_out.at[d], y_in.at[d], ry_s.at[d], ry_r.at[d], ctx_peer(z, 1 - y)
+            )
+            ry[d].start()
+            sends.append(ry[d])
+        if wait_combine and d != wait_combine[0]:
+            combine(wait_combine.pop(0))
+        done.add(step)
+        if (d, True) in done and (d, False) in done:
+            wait_combine.append(d)
+
+    all_rows = word_all.shape[0]
+    chunk = 128
+    for k in range(0, all_rows, chunk):
+        piece = word_all[k : k + chunk, :].astype(jnp.float32)
+        word_all_t[:, k : k + chunk] = piece.T.astype(jnp.bfloat16)
+
+    def ctx_term(block):
+        return jnp.dot(
+            word_all_t[:depth, :],
+            scaled_low[:, ctx_cols(block)],
+            preferred_element_type=jnp.float32,
+        )
+
+    for d in list(range(1, nx)) + [0]:
+        core_out[d] = ctx_term(xb(d) * 2 + 1 - core).astype(jnp.bfloat16)
+        rc[d] = remote(
+            core_out.at[d], core_in.at[d], rc_s.at[d], rc_r.at[d], word_peer(x, 1 - core)
+        )
+        rc[d].start()
+        sends.append(rc[d])
+        if wait_combine:
+            combine(wait_combine.pop(0))
+        ctx_part[...] = ctx_term(xb(d) * 2 + core)
+        rc[d].wait_recv()
+        total = ctx_part[...] + core_in[d].astype(jnp.float32)
+        if d == 0:
+            ctx_part[...] = total
+        else:
+            x_out[d - 1] = total.astype(jnp.bfloat16)
+            rx[d] = remote(
+                x_out.at[d - 1],
+                x_in.at[d - 1],
+                rx_s.at[d - 1],
+                rx_r.at[d - 1],
+                word_peer(xb(d), core),
+            )
+            rx[d].start()
+            sends.append(rx[d])
+    while wait_combine:
+        combine(wait_combine.pop(0))
+
+    total = ctx_part[...]
+    for d in range(1, nx):
+        rx[d].wait_recv()
+        total = total + x_in[d - 1].astype(jnp.float32)
+    ctx_out[...] = total
+    total = own_part[0]
+    for d in z_order[1:]:
+        rz[d].wait_recv()
+        total = total + z_in[d - 1].astype(jnp.float32)
+    word_out[...] = total
+    for copy in sends:
+        copy.wait_send()
+
+
+def per_device(
+    counts,
+    word_vecs,
+    word_bias,
+    word_accum,
+    word_bias_accum,
+    ctx_vecs,
+    ctx_bias,
+    ctx_accum,
+    ctx_bias_accum,
+):
+    n_word, n_ctx = lax.axis_size("word"), lax.axis_size("ctx")
+    rows, d = word_vecs.shape
+    cols = ctx_vecs.shape[0]
+    lanes = -(-(d + 2) // 128) * 128
+    depth = -(-(d + 2) // 16) * 16
+    nz, nx = n_ctx // 2, n_word // 2
+    low = jnp.bfloat16
+    word_own = jnp.concatenate(
+        [
+            word_vecs.astype(low),
+            word_bias.astype(low)[:, None],
+            jnp.ones((rows, 1), low),
+            jnp.zeros((rows, lanes - d - 2), low),
+        ],
+        axis=1,
+    )
+    ctx_own = jnp.concatenate(
+        [
+            ctx_vecs.T.astype(low),
+            jnp.ones((1, cols), low),
+            ctx_bias.astype(low)[None, :],
+            jnp.zeros((depth - d - 2, cols), low),
+        ],
+        axis=0,
+    )
+    tile_rows, tile_cols = counts.shape
+    dma = pltpu.SemaphoreType.DMA
+    vmem = pl.BlockSpec(memory_space=pltpu.VMEM)
+    word_sum, ctx_sum_t = pl.pallas_call(
+        functools.partial(tile_kernel, n_word, n_ctx),
+        out_shape=(
+            jax.ShapeDtypeStruct((rows, lanes), jnp.float32),
+            jax.ShapeDtypeStruct((depth, cols), jnp.float32),
+        ),
+        in_specs=[pl.BlockSpec(memory_space=pl.ANY), vmem, vmem],
+        out_specs=(vmem, vmem),
+        scratch_shapes=[
+            pltpu.VMEM((tile_rows, tile_cols), jnp.int32),
+            pltpu.VMEM((tile_rows, tile_cols), jnp.float32),
+            pltpu.VMEM((tile_rows, tile_cols), jnp.float32),
+            pltpu.VMEM((tile_rows, tile_cols), low),
+            pltpu.VMEM((tile_rows, lanes), low),
+            pltpu.VMEM((lanes, tile_rows), low),
+            pltpu.VMEM((lanes, tile_cols), low),
+            pltpu.VMEM((nz, rows, lanes), jnp.float32),
+            pltpu.VMEM((nz, rows, lanes), low),
+            pltpu.VMEM((nz, rows, lanes), low),
+            pltpu.VMEM((nz - 1, rows, lanes), low),
+            pltpu.VMEM((nz - 1, rows, lanes), low),
+            pltpu.VMEM((depth, cols), jnp.float32),
+            pltpu.VMEM((nx, depth, cols), low),
+            pltpu.VMEM((nx, depth, cols), low),
+            pltpu.VMEM((nx - 1, depth, cols), low),
+            pltpu.VMEM((nx - 1, depth, cols), low),
+            dma((n_ctx,)),
+            dma((nz - 1,)),
+            dma((nz - 1,)),
+            dma((nz,)),
+            dma((nz,)),
+            dma((nx - 1,)),
+            dma((nx - 1,)),
+            dma((nx,)),
+            dma((nx,)),
+            dma((nz,)),
+            dma((nz,)),
+            dma((nz - 1,)),
+            dma((nz - 1,)),
+            dma((nx,)),
+            dma((nx,)),
+            dma((nx - 1,)),
+            dma((nx - 1,)),
+        ],
+        compiler_params=pltpu.CompilerParams(
+            collective_id=0, has_side_effects=True, vmem_limit_bytes=56 * 2**20
+        ),
+    )(counts, word_own, ctx_own)
+    word_scale = 2.0 / (tile_cols * n_ctx)
+    ctx_scale = 2.0 / (tile_rows * n_word)
+    new_word_vecs, new_word_accum = adagrad(word_vecs, word_accum, word_scale * word_sum[:, :d])
+    new_word_bias, new_word_bias_accum = adagrad(
+        word_bias, word_bias_accum, word_scale * word_sum[:, d]
+    )
+    new_ctx_vecs, new_ctx_accum = adagrad(ctx_vecs, ctx_accum, ctx_scale * ctx_sum_t[:d, :].T)
+    new_ctx_bias, new_ctx_bias_accum = adagrad(
+        ctx_bias, ctx_bias_accum, ctx_scale * ctx_sum_t[d + 1, :]
+    )
+    return (
+        new_word_vecs,
+        new_word_bias,
+        new_word_accum,
+        new_word_bias_accum,
+        new_ctx_vecs,
+        new_ctx_bias,
+        new_ctx_accum,
+        new_ctx_bias_accum,
+    )
+
+
+def fits_kernel(counts, word_vecs, ctx_vecs, mesh):
+    n_word, n_ctx = mesh.shape["word"], mesh.shape["ctx"]
+    rows = word_vecs.shape[0] // (n_word * n_ctx)
+    cols = ctx_vecs.shape[0] // (n_word * n_ctx)
+    paired = n_word % 2 == 0 and n_ctx % 2 == 0 and n_word >= 4 and n_ctx >= 4
+    return paired and rows % 16 == 0 and cols % 128 == 0
+
+
 def solution(mesh):
+    def whole(counts, word_vecs, word_bias, word_accum, word_bias_accum, ctx_vecs, *rest):
+        body = per_device if fits_kernel(counts, word_vecs, ctx_vecs, mesh) else per_device_plain
+        return mapped(mesh, body)(
+            counts, word_vecs, word_bias, word_accum, word_bias_accum, ctx_vecs, *rest
+        )
+
+    return whole
+
+
+def mapped(mesh, body):
     return jax.shard_map(
-        per_device,
+        body,
         mesh=mesh,
         in_specs=(
             P("word", "ctx"),

time: 214 us -> 62.3 us (0.29)
  blocking collectives: 96.4 us -> 0 us
  waiting for transfers between devices: 63.5 us -> 0 us
  Pallas kernels: 0 us -> 48.6 us
  matrix products: 24.5 us -> 0 us
  between operations: 16.1 us -> 0.77 us
  local copies, waits for them, and re-layouts: 4.34 us -> 0.45 us
  other arithmetic: 8.66 us -> 12 us
    reduce_scatter x2 -> x0, waiting for transfers between devices: 63.5 us -> none  [the longest x1 63.4 us: per_device(): lax.psum_scatter(word_term, 'ctx', scatter_dimension=0, tiled=True)]
    pallas_call x0 -> x1, Pallas kernels: none -> 48.6 us  [per_device(): pl.pallas_call(functools.partial(tile_kernel, n_word, n_ctx), out_shape=(...]
    all_gather x3 -> x0, blocking collectives: 48.3 us -> none  [the longest x1 33.8 us: per_device(): lax.all_gather(word_vecs.astype(jnp.bfloat16), 'ctx', axis=0, tiled=True)]
    unnamed x3 -> x0, blocking collectives: 48.1 us -> none
    dot_general x3 -> x0, matrix products: 24.5 us -> none  [the longest x1 15 us: weighted_residual(): lax.dot_general(word_rows, ctx_rows, (((1,), (1,)), ((), ())), preferred_...]
    unnamed x25 -> x16, local copies, waits for them, and re-layouts: 4.33 us -> 0.04 us
  transfers between devices with their start and end apart: 2 -> 0, of which waited for: 1 -> 0; matrix products, arithmetic and copies ran while one was open for 5% -> 0% of each run, Pallas kernels for 0% -> 0%
where the time goes in v1:
time: 62.3 us; the launch traced here: 61.9 us
  Pallas kernels  48.6 us (78%)
  other arithmetic  12 us (19%)
  between operations  0.77 us (1%)
    pallas_call x1, Pallas kernels, per_device(): pl.pallas_call(functools.partial(tile_kernel, n_word, n_ctx), out_shape=(...  48.6 us
    sub x4, other arithmetic, adagrad(): return (param - step_rate * grad / jnp.sqrt(new_accum), new_accum)  5.09 us
    mul x2, other arithmetic, adagrad(): new_accum = accum + grad * grad  1.84 us

profile of v1, /device:TPU:0, one launch (start us, length us, event | category | flops | bytes accessed | tf_op | source)
XLA Modules:
  0.0 61.9 jit_solution(3295568047731238975)
XLA Ops:
  0.6 0.0 copy-start
  0.6 0.0 copy-start.4
  0.7 0.0 copy-start.1
  0.7 0.0 copy-start.6
  0.7 0.0 copy-start.5
  0.7 0.0 copy-start.7
  0.7 0.0 copy-start.2
  0.7 0.0 copy-start.3
  0.7 0.1 pad.1.clone
  0.8 1.1 %convert_bitcast_fusion = bf16[300,384]{1,0:T(8,128)(2,1)S(1)} fusion(f32[384,300]{0,1:T(8,128)} %param.14), kind=kLoop, calls=%fused_computation.6 | loop fusion | flops 115200 | bytes 691200 | tf_op jit(solution)/shard_map/convert_element_type | solution.py:425
  1.9 0.7 %convert_element_type.19 = bf16[384]{0:T(512)(128)(2,1)S(1)} convert(f32[384]{0:T(512)} %param.15) | non-fusion elementwise | flops 384 | bytes 2304 | tf_op jit(solution)/shard_map/convert_element_type | solution.py:427
  2.6 0.1 pad.3.clone
  2.7 0.8 %maximum_maximum_fusion.ctx_own = bf16[304,384]{1,0:T(8,128)(2,1)} fusion(bf16[1,384]{1,0:T(2,128)(2,1)S(1)} %broadcast_in_dim.22, bf16[300,384]{1,0:T(8,128)(2,1)S(1)} %convert_bitcast_fusion, bf16[304]{0:T(512)(128)(2,1)S(1)} %pad.3.clone, bf16[304]{0:T(512)(128)(2,1)S(1)} %pad.1.clone), kind=kLoop, calls=%fused_computation.5 | loop fusion | flops 933888 | bytes 465856 | tf_op jit(solution)/shard_map/concatenate | solution.py:423
  3.6 0.1 pad.6.clone
  3.6 1.0 %convert_element_type.15 = bf16[192,300]{1,0:T(8,128)(2,1)S(1)} convert(f32[192,300]{1,0:T(8,128)} %param.10) | non-fusion elementwise | flops 57600 | bytes 345600 | tf_op jit(solution)/shard_map/convert_element_type | solution.py:416
  4.6 0.7 %convert_element_type.16 = bf16[192]{0:T(256)(128)(2,1)S(1)} convert(f32[192]{0:T(256)} %param.11) | non-fusion elementwise | flops 192 | bytes 1152 | tf_op jit(solution)/shard_map/convert_element_type | solution.py:417
  5.3 0.1 broadcast_in_dim.24
  5.4 0.1 pad.7.clone
  5.5 0.8 %maximum_maximum_fusion.1.word_own = bf16[192,384]{1,0:T(8,128)(2,1)} fusion(bf16[192,1]{1,0:T(8,128)(2,1)S(1)} %broadcast_in_dim.24, bf16[192,300]{1,0:T(8,128)(2,1)S(1)} %convert_element_type.15, bf16[384]{0:T(512)(128)(2,1)S(1)} %pad.7.clone, bf16[384]{0:T(512)(128)(2,1)S(1)} %pad.6.clone), kind=kLoop, calls=%fused_computation.7 | loop fusion | flops 589824 | bytes 264576 | tf_op jit(solution)/shard_map/concatenate | solution.py:414
  6.3 48.6 %shard_map.152 = (f32[192,384]{1,0:T(8,128)}, f32[304,384]{1,0:T(8,128)}) custom-call(s32[1536,1536]{1,0:T(8,128)} %counts_hbm.1, bf16[192,384]{1,0:T(8,128)(2,1)} %maximum_maximum_fusion.1.word_own, bf16[304,384]{1,0:T(8,128)(2,1)} %maximum_maximum_fusion.ctx_own), custom_call_target="tpu_custom_call" | custom-call | tf_op jit(solution)/shard_map/pallas_call | solution.py:435
  54.9 0.7 %multiply_reduce_fusion.2 = (f32[384]{0:T(512)S(1)}, f32[384]{0:T(512)S(1)}) fusion(f32[304,384]{1,0:T(8,128)} %get-tuple-element.11), kind=kLoop, calls=%fused_computation.11 | loop fusion | flops 1152 | bytes 4608 | tf_op jit(solution)/shard_map/mul | solution.py:27
  55.6 0.0 copy-done.4
  55.6 0.0 copy-done.5
  55.6 0.6 multiply_subtract_fusion.1
  56.2 1.1 %multiply_reduce_fusion = (f32[192]{0:T(256)S(1)}, f32[192]{0:T(256)S(1)}) fusion(f32[192,384]{1,0:T(8,128)} %get-tuple-element.10), kind=kLoop, calls=%fused_computation.8 | loop fusion | flops 576 | bytes 2304 | tf_op jit(solution)/shard_map/mul | solution.py:27
  57.3 0.0 copy-done.6
  57.3 0.0 copy-done.7
  57.4 0.6 multiply_subtract_fusion.2
  57.9 0.0 copy-done.2
  57.9 2.1 %fusion = (f32[384,300]{0,1:T(8,128)}, f32[384,300]{0,1:T(8,128)}) fusion(f32[384,300]{0,1:T(8,128)S(1)} %copy-done, f32[304,384]{1,0:T(8,128)} %get-tuple-element.11, f32[384,300]{0,1:T(8,128)S(1)} %copy-done.2), kind=kLoop, calls=%fused_computation.2 | loop fusion | flops 691200 | bytes 2304000 | tf_op jit(solution)/shard_map/sub | solution.py:28
  60.0 0.0 copy-done.3
  60.0 1.8 %multiply_subtract_fusion = (f32[192,300]{1,0:T(8,128)}, f32[192,300]{1,0:T(8,128)}) fusion(f32[192,300]{1,0:T(8,128)S(1)} %copy-done.1, f32[192,384]{1,0:T(8,128)} %get-tuple-element.10, f32[192,300]{1,0:T(8,128)S(1)} %copy-done.3), kind=kLoop, calls=%fused_computation.3 | loop fusion | flops 345600 | bytes 1152000 | tf_op jit(solution)/shard_map/sub | solution.py:28
  (5 shorter events, 0.0 us)
Async XLA Ops:
  0.6 57.3 %copy-start = (f32[384,300]{0,1:T(8,128)S(1)}, f32[384,300]{0,1:T(8,128)}, u32[]{:S(2)}) copy-start(f32[384,300]{0,1:T(8,128)} %param.14) | copy-start | bytes 1382404
  0.6 55.0 %copy-start.4 = (f32[384]{0:T(512)S(1)}, f32[384]{0:T(512)}, u32[]{:S(2)}) copy-start(f32[384]{0:T(512)} %param.15) | copy-start | bytes 4612
  0.7 59.4 %copy-start.1 = (f32[192,300]{1,0:T(8,128)S(1)}, f32[192,300]{1,0:T(8,128)}, u32[]{:S(2)}) copy-start(f32[192,300]{1,0:T(8,128)} %param.10) | copy-start | bytes 691204
  0.7 56.7 %copy-start.6 = (f32[192]{0:T(256)S(1)}, f32[192]{0:T(256)}, u32[]{:S(2)}) copy-start(f32[192]{0:T(256)} %param.11) | copy-start | bytes 2308
  0.7 54.9 %copy-start.5 = (f32[384]{0:T(512)S(1)}, f32[384]{0:T(512)}, u32[]{:S(2)}) copy-start(f32[384]{0:T(512)} %param.17) | copy-start | bytes 4612
  0.7 56.7 %copy-start.7 = (f32[192]{0:T(256)S(1)}, f32[192]{0:T(256)}, u32[]{:S(2)}) copy-start(f32[192]{0:T(256)} %param.13) | copy-start | bytes 2308
  0.7 57.2 %copy-start.2 = (f32[384,300]{0,1:T(8,128)S(1)}, f32[384,300]{0,1:T(8,128)}, u32[]{:S(2)}) copy-start(f32[384,300]{0,1:T(8,128)} %param.16) | copy-start | bytes 1382404
  0.7 59.3 %copy-start.3 = (f32[192,300]{1,0:T(8,128)S(1)}, f32[192,300]{1,0:T(8,128)}, u32[]{:S(2)}) copy-start(f32[192,300]{1,0:T(8,128)} %param.12) | copy-start | bytes 691204

commit v2 on v1

--- a/solution.py
+++ b/solution.py
@@ -113,8 +113,10 @@
     n_word,
     n_ctx,
     counts_hbm,
-    word_own,
-    ctx_own,
+    word_vecs,
+    word_bias,
+    ctx_vecs_t,
+    ctx_bias,
     word_out,
     ctx_out,
     counts,
@@ -152,8 +154,9 @@
     rx_s,
     rx_r,
 ):
-    rows, lanes = word_own.shape
-    depth, cols = ctx_own.shape
+    rows, lanes = word_out.shape
+    depth, cols = ctx_out.shape
+    dim = word_vecs.shape[1]
     nz, nx = n_ctx // 2, n_word // 2
     w, c = lax.axis_index("word"), lax.axis_index("ctx")
     x, core = w // 2, w % 2
@@ -205,6 +208,22 @@
     peers += [word_peer(xf(d), core) for d in range(1, nx)] + [word_peer(x, 1 - core)]
     for peer in peers:
         pl.semaphore_signal(barrier, inc=1, device_id=peer, device_id_type=MESH)
+    base = dim // 128 * 128
+    at_own = word_rows(c)
+    lane = lax.broadcasted_iota(jnp.int32, (rows, lanes - base), 1) + base
+    column = jnp.broadcast_to(word_bias[...], (128, rows)).T
+    own_part[0, :, base:] = jnp.where(lane == dim, column, jnp.where(lane == dim + 1, 1.0, 0.0))
+    own_part[0, :, :dim] = word_vecs[...]
+    word_all[at_own, :] = own_part[0].astype(jnp.bfloat16)
+    ctx_part[:dim, :] = ctx_vecs_t[...]
+    ctx_part[dim : dim + 1, :] = jnp.ones((1, cols), jnp.float32)
+    ctx_part[dim + 1 : dim + 2, :] = ctx_bias[...]
+    ctx_part[dim + 2 :, :] = jnp.zeros((depth - dim - 2, cols), jnp.float32)
+    ctx_all[:depth, ctx_cols(w)] = ctx_part[...].astype(jnp.bfloat16)
+    ctx_all[depth:, :] = jnp.zeros((lanes - depth, ctx_all.shape[1]), ctx_all.dtype)
+    word_own = word_all.at[at_own, :]
+    ctx_own = ctx_all.at[:depth, ctx_cols(w)]
+
     pl.semaphore_wait(barrier, len(peers))
 
     sends = []
@@ -246,22 +265,10 @@
         )
         wz[d].start()
         sends.append(wz[d])
-    word_all[word_rows(c), :] = word_own[...]
-    ctx_all[:depth, ctx_cols(w)] = ctx_own[...]
-    ctx_all[depth:, :] = jnp.zeros((lanes - depth, ctx_all.shape[1]), ctx_all.dtype)
-
-    forwards = [("c", d) for d in range(1, nx)] + [("w", d) for d in z_order[1:]]
-
-    def forward():
-        if not forwards:
-            return
-        kind, d = forwards.pop(0)
-        if kind == "c":
-            cx[d].wait_recv()
-            cc_copy(d, ctx_all.at[:depth, ctx_cols(xb(d) * 2 + core)])
-        else:
-            wz[d].wait_recv()
-            wy_copy(d, word_all.at[word_rows(zb(d) * 2 + y), :])
+
+    def forward_word(d):
+        wz[d].wait_recv()
+        wy_copy(d, word_all.at[word_rows(zb(d) * 2 + y), :])
 
     group = 16
     log2_cap = math.log2(count_cap)
@@ -278,10 +285,12 @@
             weight[at, :] = jnp.where(tile > 0, power, 0.0)
             log_count[at, :] = log2 * math.log(2.0)
 
-        if i >= 2:
-            forward()
-    while forwards:
-        forward()
+        if i == len(steps) // 2:
+            for d in range(1, nx):
+                cx[d].wait_recv()
+                cc_copy(d, ctx_all.at[:depth, ctx_cols(xb(d) * 2 + core)])
+    forward_word(z_order[1])
+    pending = z_order[2:]
     for d in range(nx):
         cc[d].wait_recv()
 
@@ -309,6 +318,8 @@
     for step in steps:
         d, mine = step
         at = word_rows(block_of(step))
+        if pending and len(done) >= 1:
+            forward_word(pending.pop(0))
         if not mine:
             wy[d].wait_recv()
         block = word_all[at, :]
@@ -393,6 +404,20 @@
         copy.wait_send()
 
 
+def update_kernel(word_scale, ctx_scale, word_sum, ctx_sum_t, *refs):
+    params, accums, outs = refs[:4], refs[4:8], refs[8:]
+    dim = params[0].shape[1]
+    base = dim // 128 * 128
+    sums = (
+        word_scale * word_sum[:, :dim],
+        word_scale * word_sum[:, base:].T[dim - base : dim - base + 1, :],
+        ctx_scale * ctx_sum_t[:dim, :],
+        ctx_scale * ctx_sum_t[dim + 1 : dim + 2, :],
+    )
+    for i, grad in enumerate(sums):
+        outs[i][...], outs[4 + i][...] = adagrad(params[i][...], accums[i][...], grad)
+
+
 def per_device(
     counts,
     word_vecs,
@@ -411,24 +436,6 @@
     depth = -(-(d + 2) // 16) * 16
     nz, nx = n_ctx // 2, n_word // 2
     low = jnp.bfloat16
-    word_own = jnp.concatenate(
-        [
-            word_vecs.astype(low),
-            word_bias.astype(low)[:, None],
-            jnp.ones((rows, 1), low),
-            jnp.zeros((rows, lanes - d - 2), low),
-        ],
-        axis=1,
-    )
-    ctx_own = jnp.concatenate(
-        [
-            ctx_vecs.T.astype(low),
-            jnp.ones((1, cols), low),
-            ctx_bias.astype(low)[None, :],
-            jnp.zeros((depth - d - 2, cols), low),
-        ],
-        axis=0,
-    )
     tile_rows, tile_cols = counts.shape
     dma = pltpu.SemaphoreType.DMA
     vmem = pl.BlockSpec(memory_space=pltpu.VMEM)
@@ -438,7 +445,7 @@
             jax.ShapeDtypeStruct((rows, lanes), jnp.float32),
             jax.ShapeDtypeStruct((depth, cols), jnp.float32),
         ),
-        in_specs=[pl.BlockSpec(memory_space=pl.ANY), vmem, vmem],
+        in_specs=[pl.BlockSpec(memory_space=pl.ANY), vmem, vmem, vmem, vmem],
         out_specs=(vmem, vmem),
         scratch_shapes=[
             pltpu.VMEM((tile_rows, tile_cols), jnp.int32),
@@ -479,26 +486,36 @@
         compiler_params=pltpu.CompilerParams(
             collective_id=0, has_side_effects=True, vmem_limit_bytes=56 * 2**20
         ),
-    )(counts, word_own, ctx_own)
+    )(counts, word_vecs, word_bias[None, :], ctx_vecs.T, ctx_bias[None, :])
     word_scale = 2.0 / (tile_cols * n_ctx)
     ctx_scale = 2.0 / (tile_rows * n_word)
-    new_word_vecs, new_word_accum = adagrad(word_vecs, word_accum, word_scale * word_sum[:, :d])
-    new_word_bias, new_word_bias_accum = adagrad(
-        word_bias, word_bias_accum, word_scale * word_sum[:, d]
-    )
-    new_ctx_vecs, new_ctx_accum = adagrad(ctx_vecs, ctx_accum, ctx_scale * ctx_sum_t[:d, :].T)
-    new_ctx_bias, new_ctx_bias_accum = adagrad(
-        ctx_bias, ctx_bias_accum, ctx_scale * ctx_sum_t[d + 1, :]
+    shapes = [(rows, d), (1, rows), (d, cols), (1, cols)]
+    outs = pl.pallas_call(
+        functools.partial(update_kernel, word_scale, ctx_scale),
+        out_shape=tuple(jax.ShapeDtypeStruct(shape, jnp.float32) for shape in shapes * 2),
+        in_specs=[vmem] * 10,
+        out_specs=(vmem,) * 8,
+    )(
+        word_sum,
+        ctx_sum_t,
+        word_vecs,
+        word_bias[None, :],
+        ctx_vecs.T,
+        ctx_bias[None, :],
+        word_accum,
+        word_bias_accum[None, :],
+        ctx_accum.T,
+        ctx_bias_accum[None, :],
     )
     return (
-        new_word_vecs,
-        new_word_bias,
-        new_word_accum,
-        new_word_bias_accum,
-        new_ctx_vecs,
-        new_ctx_bias,
-        new_ctx_accum,
-        new_ctx_bias_accum,
+        outs[0],
+        outs[1][0],
+        outs[4],
+        outs[5][0],
+        outs[2].T,
+        outs[3][0],
+        outs[6].T,
+        outs[7][0],
     )
 
 
@@ -507,7 +524,8 @@
     rows = word_vecs.shape[0] // (n_word * n_ctx)
     cols = ctx_vecs.shape[0] // (n_word * n_ctx)
     paired = n_word % 2 == 0 and n_ctx % 2 == 0 and n_word >= 4 and n_ctx >= 4
-    return paired and rows % 16 == 0 and cols % 128 == 0
+    packed = 0 < word_vecs.shape[1] % 128 <= 126
+    return paired and packed and rows % 16 == 0 and cols % 128 == 0
 
 
 def solution(mesh):

time: 62.3 us -> 56.8 us (0.912)
  other arithmetic: 12 us -> 2.53 us
  Pallas kernels: 48.6 us -> 50.9 us
  local copies, waits for them, and re-layouts: 0.45 us -> 2.49 us
    sub x4 -> x0, other arithmetic: 5.09 us -> none  [adagrad(): return (param - step_rate * grad / jnp.sqrt(new_accum), new_accum)]
    convert_element_type x4 -> x0, other arithmetic: 3.5 us -> none  [the longest x1 1.15 us: per_device(): ctx_vecs.T.astype(low)]
    pallas_call x0 -> x1, Pallas kernels: none -> 3.04 us  [per_device(): pl.pallas_call(functools.partial(update_kernel, word_scale, ctx_scale), o...]
    pallas_call x0 -> x2, other arithmetic: none -> 2.53 us  [per_device(): pl.pallas_call(functools.partial(update_kernel, word_scale, ctx_scale), o...]
    broadcast_in_dim x4 -> x2, local copies, waits for them, and re-layouts: 0.1 us -> 2.49 us  [the longest x1 1.25 us: per_device(): ctx_bias[None, :]]
    mul x2 -> x0, other arithmetic: 1.84 us -> none  [adagrad(): new_accum = accum + grad * grad]
    concatenate x2 -> x0, other arithmetic: 1.6 us -> none  [the longest x1 0.85 us: per_device(): jnp.concatenate([ctx_vecs.T.astype(low), jnp.ones((1, cols), low), ctx_bi...]
    pallas_call x1, Pallas kernels: 48.6 us -> 47.9 us  [per_device(): pl.pallas_call(functools.partial(tile_kernel, n_word, n_ctx), out_shape=(...]
where the time goes in v2:
time: 56.8 us; the launch traced here: 56.6 us
  Pallas kernels  50.9 us (90%)
  other arithmetic  2.53 us (4%)
  local copies, waits for them, and re-layouts  2.49 us (4%)
  between operations  0.65 us (1%)
    pallas_call x1, Pallas kernels, per_device(): pl.pallas_call(functools.partial(tile_kernel, n_word, n_ctx), out_shape=(...  47.9 us
    pallas_call x1, Pallas kernels, per_device(): pl.pallas_call(functools.partial(update_kernel, word_scale, ctx_scale), o...  3.04 us
    pallas_call x2, other arithmetic, per_device(): pl.pallas_call(functools.partial(update_kernel, word_scale, ctx_scale), o...  2.53 us
    broadcast_in_dim x1, local copies, waits for them, and re-layouts, per_device(): ctx_bias[None, :]  1.25 us
    broadcast_in_dim x1, local copies, waits for them, and re-layouts, per_device(): ctx_bias_accum[None, :]  1.24 us

profile of v2, /device:TPU:0, one launch (start us, length us, event | category | flops | bytes accessed | tf_op | source)
XLA Modules:
  0.0 56.6 jit_solution(4906996838411509812)
XLA Ops:
  0.6 1.2 %broadcast_in_dim.15.ctx_bias.refs_3_ = f32[1,384]{1,0:T(1,128)} reshape(f32[384]{0:T(512)} %param.15) | data formatting | bytes 3072 | tf_op jit(solution)/shard_map/broadcast_in_dim | solution.py:489
  1.9 1.2 %broadcast_in_dim.17.refs_7_ = f32[1,384]{1,0:T(1,128)} reshape(f32[384]{0:T(512)} %param.17) | data formatting | bytes 3072 | tf_op jit(solution)/shard_map/broadcast_in_dim | solution.py:508
  3.1 47.9 %shard_map.152 = (f32[192,384]{1,0:T(8,128)}, f32[304,384]{1,0:T(8,128)}) custom-call(s32[1536,1536]{1,0:T(8,128)} %counts_hbm.1, f32[192,300]{1,0:T(8,128)} %refs_0_.1, f32[1,192]{1,0:T(1,128)} %bitcast.11, f32[300,384]{1,0:T(8,128)} %bitcast.8, f32[1,384]{1,0:T(1,128)} %broadcast_in_dim.15.ctx_bias.refs_3_), custom_call_target="tpu_custom_call" | custom-call | tf_op jit(solution)/shard_map/pallas_call | solution.py:442
  51.0 3.0 %shard_map.153 = (f32[192,300]{1,0:T(8,128)}, f32[1,192]{1,0:T(1,128)}, f32[300,384]{1,0:T(8,128)}, f32[1,384]{1,0:T(1,128)}, f32[192,300]{1,0:T(8,128)}, /*inde...) custom-call(f32[192,384]{1,0:T(8,128)} %get-tuple-element.18.word_sum, f32[304,384]{1,0:T(8,128)} %get-tuple-element.19.ctx_sum_t, ...), custom_call_target="tpu_custom_call" | custom-call | tf_op jit(solution)/shard_map/pallas_call | solution.py:493
  54.0 1.3 %reduce = f32[384]{0:T(512)} reduce(f32[1,384]{1,0:T(1,128)} %get-tuple-element.25, f32[]{:T(128)} %constant), dimensions={0}, to_apply=%get-tuple-element.25.reduce_sub_computation | reduce | bytes 3076 | tf_op jit(solution)/shard_map/pallas_call | solution.py:493
  55.3 1.3 %reduce.1 = f32[384]{0:T(512)} reduce(f32[1,384]{1,0:T(1,128)} %get-tuple-element.27, f32[]{:T(128)} %constant), dimensions={0}, to_apply=%get-tuple-element.27.reduce_sub_computation | reduce | bytes 3076 | tf_op jit(solution)/shard_map/pallas_call | solution.py:493
